TPU v7x, 256 devices: a whole 4x4x8 slice. The times are simulated.
256 devices in a mesh: seq: 32 (over y, x, core), head: 8 (over z).
Axes of the slice: x: 4, y: 4, z: 8, core: 2. Of those that a mesh axis runs over, the one named last changes fastest.
Arguments:
- q_values: bfloat16 [65536, 4096], P('seq', 'head'), may hold values from -6 to 6
- k_values: bfloat16 [65536, 4096], P('seq', 'head'), may hold values from -6 to 6
- v_values: bfloat16 [65536, 4096], P('seq', 'head'), may hold values from -6 to 6
- q_scales: float32 [65536, 32], P('seq', 'head'), may hold values from 0.5 to 4
- k_scales: float32 [65536, 32], P('seq', 'head'), may hold values from 0.5 to 4
- v_scales: float32 [65536, 32], P('seq', 'head'), may hold values from 0.5 to 2
- conv_weight: float32 [32, 33], P('head'), may hold values from -0.9 to 0.9
Outputs:
- attended: bfloat16 [65536, 4096], P('seq', 'head')
All inputs are finite; a program needn't handle non-finite values.
Results may differ from a plain program's by a relative error of at most 0.03.
Values may be sent and summed in bfloat16 or wider, within the bound.
A program may use at most 128 MiB of HBM per device.

v0:
```python
import functools
import jax
import jax.numpy as jnp
from jax import lax
from jax.sharding import Mesh
from jax.sharding import PartitionSpec as P

HEAD_DIM = 128
LANDMARKS = 256
SWEEPS = 6
SEQ = ("seq_0", "seq_1", "seq_2")


def side_by_side(arrays, axis, dim, along):
    both = jnp.concatenate(arrays, axis=along)
    result, at, finished = (lax.all_gather(both, axis, axis=dim, tiled=True), 0, [])
    for a in arrays:
        finished.append(lax.slice_in_dim(result, at, at + a.shape[along], axis=along))
        at += a.shape[along]
    return tuple(finished)


def from_everyone(shard, axis):
    copies = jnp.broadcast_to(shard, (lax.axis_size(axis), *shard.shape))
    return lax.all_to_all(copies, axis, split_axis=0, concat_axis=0, tiled=True)


def taken_together(shard, axis):
    everything = from_everyone(shard, axis)
    return jnp.max(everything, axis=0)


def packed_total(arrays, axis):
    line, at, finished = (jnp.concatenate([a.reshape(-1) for a in arrays]), 0, [])
    total = taken_together(line, axis)
    for a in arrays:
        finished.append(total[at : at + a.size].reshape(a.shape))
        at += a.size
    return tuple(finished)


def by_axis(shard, axes):
    return functools.reduce(lax.pmax, axes, shard)


def padded_2(shard, sides, width):
    for axis, dim in sides:
        count, length = (lax.axis_size(axis), shard.shape[dim])
        up = [(i, (i + 1) % count) for i in range(count - 1)]
        down = [(j, i) for i, j in up]
        last = lax.slice_in_dim(shard, length - width, length, axis=dim)
        leading = lax.slice_in_dim(shard, 0, width, axis=dim)
        before = lax.ppermute(last, axis, up)
        after = lax.ppermute(leading, axis, down)
        shard = jnp.concatenate([before, shard, after], axis=dim)
    return shard


def dequant(value_rows, scales):
    count = scales.shape[1]
    shaped = value_rows.reshape(value_rows.shape[0], count, HEAD_DIM).astype(jnp.float32)
    return (shaped * scales[:, :, None]).astype(jnp.bfloat16)


def newton(kernel, initial, right_side):
    eye_matrix = jnp.eye(kernel.shape[0], dtype=jnp.float32)
    iterate = initial
    for sweep in range(SWEEPS):
        product = jnp.dot(kernel, iterate)
        inner_term = 7.0 * eye_matrix - product
        inner_term = 15.0 * eye_matrix - jnp.dot(product, inner_term)
        inner_term = 13.0 * eye_matrix - jnp.dot(product, inner_term)
        iterate = 0.25 * jnp.dot(iterate, inner_term)
    return jnp.dot(iterate, right_side).astype(jnp.bfloat16)


def shards(q_values, k_values, v_values, q_scales, k_scales, v_scales, conv_weight):
    tok_rows = q_values.shape[0]
    head_count = q_scales.shape[1]
    seq_count = lax.axis_size(SEQ)
    marks_here = LANDMARKS // seq_count
    segment = tok_rows // marks_here
    query_rows = dequant(q_values, q_scales)
    key_rows = dequant(k_values, k_scales)
    value_rows = dequant(v_values, v_scales)

    def means(source):
        shaped = source.reshape(marks_here, segment, head_count, HEAD_DIM).astype(jnp.float32)
        return (
            jnp.mean(shaped, axis=1).astype(jnp.bfloat16).reshape(marks_here, head_count * HEAD_DIM)
        )

    query_landmarks, key_landmarks = side_by_side((means(query_rows), means(key_rows)), SEQ, 0, 1)
    query_landmarks = query_landmarks.reshape(LANDMARKS, head_count, HEAD_DIM)
    key_landmarks = key_landmarks.reshape(LANDMARKS, head_count, HEAD_DIM)
    pseudo_inverse_factor = HEAD_DIM ** (-0.5)
    landmark_kernel = (
        jnp.einsum(
            "jvc,kvc->vjk", query_landmarks, key_landmarks, preferred_element_type=jnp.float32
        )
        * pseudo_inverse_factor
    )
    middle = jax.nn.softmax(landmark_kernel, axis=-1)
    col_top = jnp.max(jnp.sum(middle, axis=1))
    row_top = jnp.max(jnp.sum(middle, axis=2))
    col_top, row_top = packed_total((col_top, row_top), "head")
    start = jnp.swapaxes(middle, 1, 2) / (col_top * row_top)
    distant_term = (
        jnp.einsum("kli,nli->lkn", query_landmarks, key_rows, preferred_element_type=jnp.float32)
        * pseudo_inverse_factor
    )
    far_top = by_axis(jnp.max(distant_term, axis=-1), SEQ)
    weight_matrix = jnp.exp(distant_term - far_top[:, :, None])
    total = jnp.sum(weight_matrix, axis=-1)
    summed = jnp.einsum(
        "lnx,xlj->nlj",
        weight_matrix.astype(jnp.bfloat16),
        value_rows,
        preferred_element_type=jnp.float32,
    )
    total, summed = (
        lax.psum(total.astype(jnp.bfloat16), SEQ).astype(jnp.float32),
        lax.psum(summed.astype(jnp.bfloat16), SEQ).astype(jnp.float32),
    )
    reduced = summed / jnp.swapaxes(total, 0, 1)[:, :, None]
    projected_values = jax.vmap(newton, in_axes=(0, 0, 1), out_axes=1)(middle, start, reduced)
    near_scores = (
        jnp.einsum("zea,uea->ezu", query_rows, key_landmarks, preferred_element_type=jnp.float32)
        * pseudo_inverse_factor
    )
    local_term = jax.nn.softmax(near_scores, axis=-1).astype(jnp.bfloat16)
    attended = jnp.einsum(
        "kbv,vkg->bkg", local_term, projected_values, preferred_element_type=jnp.float32
    ).reshape(tok_rows, head_count * HEAD_DIM)
    flat_values = value_rows.reshape(tok_rows, head_count * HEAD_DIM)
    tap_count = conv_weight.shape[1]
    padded = padded_2(flat_values, ((SEQ, 0),), tap_count // 2)
    tap_table = jnp.repeat(conv_weight, HEAD_DIM, axis=0)
    mixed = jnp.zeros((tok_rows, head_count * HEAD_DIM), jnp.float32)
    for tap_index in range(tap_count):
        mixed = (
            mixed
            + padded[tap_index : tap_index + tok_rows].astype(jnp.float32) * tap_table[:, tap_index]
        )
    return (attended + mixed).astype(jnp.bfloat16)


def solution(mesh):
    finer = Mesh(
        mesh.devices.reshape(4, 4, 2, mesh.shape["head"]), ("seq_0", "seq_1", "seq_2", "head")
    )
    placed = (
        P(SEQ, "head"),
        P(SEQ, "head"),
        P(SEQ, "head"),
        P(SEQ, "head"),
        P(SEQ, "head"),
        P(SEQ, "head"),
        P("head", None),
    )
    return jax.shard_map(
        shards, mesh=finer, in_specs=placed, out_specs=P(SEQ, "head"), check_vma=False
    )
```

profile of v0, /device:TPU:32, one launch (start us, length us, event | category | flops | bytes accessed | tf_op | source)
XLA Modules:
  0.0 302.6 jit_solution(4559212239840184039)
XLA Ops:
  6.5 4.7 %reshape.126 = f32[8,256,4,128]{3,2,1,0:T(4,128)} reshape(bf16[2048,512]{1,0:T(8,128)(2,1)} %param.7) | data formatting | bytes 6291456 | tf_op jit(solution)/shard_map/convert_element_type | solution.py:61
  11.7 4.6 %convert_reduce_fusion.1 = f32[8,4,128]{2,1,0:T(4,128)S(1)} fusion(f32[8,256,4,128]{3,2,1,0:T(4,128)} %reshape.126, f32[8,256,4]{2,1,0:T(8,128)S(1)} %bitcast.119), kind=kLoop, calls=%fused_computation.52 | loop fusion | flops 4190208 | bytes 4243456 | tf_op jit(solution)/shard_map/reduce_sum | solution.py:90
  16.3 3.0 reshape.127
  19.6 4.4 %convert_reduce_fusion = f32[8,4,128]{2,1,0:T(4,128)S(1)} fusion(f32[8,256,4,128]{3,2,1,0:T(4,128)} %reshape.127, f32[8,256,4]{2,1,0:T(8,128)S(1)} %bitcast.120), kind=kLoop, calls=%fused_computation.50 | loop fusion | flops 4190208 | bytes 4243456 | tf_op jit(solution)/shard_map/reduce_sum | solution.py:90
  24.1 25.1 %all_gather.3 = bf16[256,1024]{1,0:T(8,128)(2,1)S(1)} all-gather(bf16[8,1024]{1,0:T(8,128)(2,1)S(1)} %pad_maximum_fusion.2), channel_id=1, replica_groups=mesh['seq_0'=4,'seq_1'=4,'seq_2'=2,'head'=8] {'seq_0','seq_1','seq_2'}, dimensions={0}, use_global_device_ids=true | all-gather | bytes 540672 | tf_op jit(solution)/shard_map/all_gather | solution.py:16
  55.7 8.6 %all-to-all-start = ((f32[8,1,2]{2,1,0:T(1,128)}), f32[8,1,2]{2,1,0:T(1,128)S(1)}, u32[]{:S(2)}, u32[]{:S(2)}) async-start(f32[8,1,2]{2,1,0:T(1,128)} %broadcast_in_dim.4), calls=%async_computation | async-start | bytes 8192 | tf_op jit(solution)/shard_map/all_to_all | solution.py:25
  64.3 4.4 %multiply_reduce_fusion = (f32[4,256]{1,0:T(4,128)S(1)}, f32[4,256,2048]{2,1,0:T(8,128)}) fusion(bf16[256,4,128]{0,2,1:T(8,128)(2,1)S(1)} %bitcast.123, f32[2048,4]{0,1:T(4,128)S(1)} %copy-done.11, bf16[2048,512]{1,0:T(8,128)(2,1)S(1)} %copy-done.4), kind=kOutput, calls=%fused_computation.34 | convolution fusion | flops 544209920 | bytes 10784768 | tf_op jit(solution)/shard_map/kli,nli->lkn/dot_general | solution.py:109
  68.7 10.2 %pmax.21 = f32[4,256]{1,0:T(4,128)S(1)} all-reduce(f32[4,256]{1,0:T(4,128)S(1)} %get-tuple-element.48), channel_id=1, replica_groups=mesh['seq_0'=4,'seq_1'=4,'seq_2'=2,'head'=8] {'seq_0'}, use_global_device_ids=true, to_apply=%region_10.0 | all-reduce | flops 1024 | bytes 8192 | tf_op jit(solution)/shard_map/pmax | solution.py:43
  78.9 8.5 %pmax.22 = f32[4,256]{1,0:T(4,128)S(1)} all-reduce(f32[4,256]{1,0:T(4,128)S(1)} %pmax.21), channel_id=1, replica_groups=mesh['seq_0'=4,'seq_1'=4,'seq_2'=2,'head'=8] {'seq_1'}, use_global_device_ids=true, to_apply=%region_11.0 | all-reduce | flops 1024 | bytes 8192 | tf_op jit(solution)/shard_map/pmax | solution.py:43
  90.0 4.1 %copy.106 = f32[2048,512]{0,1:T(8,128)} copy(bf16[2048,512]{1,0:T(8,128)(2,1)} %param.9) | data formatting | bytes 6291456 | tf_op jit(solution)/shard_map/convert_element_type | solution.py:61
  94.1 2.7 multiply_convert_fusion.1
  96.8 5.9 %fusion.121 = bf16[256,4,128]{0,2,1:T(8,128)(2,1)} fusion(bf16[2048,4,128]{0,2,1:T(8,128)(2,1)S(1)} %multiply_convert_fusion.1, f32[4,256,2048]{2,1,0:T(8,128)} %get-tuple-element.49, f32[4,256]{1,0:T(4,128)S(1)} %pmax.23), kind=kOutput, calls=%fused_computation.148 | convolution fusion | flops 543293440 | bytes 10752000 | tf_op jit(solution)/shard_map/lnx,xlj->nlj/dot_general | solution.py:115
  106.6 4.4 %fusion.2 = bf16[4,256]{1,0:T(4,128)(2,1)S(1)} fusion(f32[4,256,2048]{2,1,0:T(8,128)} %get-tuple-element.49, f32[4,256]{1,0:T(4,128)S(1)} %pmax.23), kind=kLoop, calls=%fused_computation.37 | loop fusion | flops 6290432 | bytes 8394752 | tf_op jit(solution)/shard_map/reduce_sum | solution.py:114
  111.1 4.2 %fusion.16 = f32[4,2048,256]{1,2,0:T(8,128)} fusion(bf16[256,4,128]{0,2,1:T(8,128)(2,1)S(1)} %bitcast.125, f32[2048,4]{0,1:T(4,128)S(1)} %copy-done.12, bf16[2048,512]{1,0:T(8,128)(2,1)S(1)} %copy-done.5), kind=kOutput, calls=%fused_computation.56 | convolution fusion | flops 540016640 | bytes 10780672 | tf_op jit(solution)/shard_map/zea,uea->ezu/dot_general | solution.py:128
  116.9 11.7 %fusion.170 = (f32[4,2048]{1,0:T(4,128)S(1)}, f32[4,2048,256]{1,2,0:T(8,128)}) fusion(f32[4,2048,256]{1,2,0:T(8,128)} %fusion.16), kind=kOutput, calls=%fused_computation.199 | output fusion | flops 8388863 | bytes 16809984 | tf_op jit(solution)/shard_map/sub | solution.py:131
  128.6 2.5 mul.490
  131.1 5.3 %copy.108 = f32[2048,512]{1,0:T(8,128)} copy(f32[2048,512]{0,1:T(8,128)} %bitcast.118) | data formatting | bytes 8388608 | tf_op jit(solution)/shard_map/mul | solution.py:62
  136.5 4.9 %multiply_convert_fusion = bf16[2048,512]{1,0:T(8,128)(2,1)} fusion(f32[2048,512]{1,0:T(8,128)} %copy.108, bf16[2048,512]{1,0:T(8,128)(2,1)} %param.9), kind=kLoop, calls=%fused_computation.45 | loop fusion | flops 3145728 | bytes 8388608 | tf_op jit(solution)/shard_map/convert_element_type | solution.py:62
  141.4 64.7 %psum.15 = bf16[256,4]{0,1:T(4,128)(2,1)S(1)} all-reduce(bf16[256,4]{0,1:T(4,128)(2,1)S(1)} %bitcast.164), channel_id=1, replica_groups=mesh['seq_0'=4,'seq_1'=4,'seq_2'=2,'head'=8] {'seq_0','seq_1','seq_2'}, use_global_device_ids=true, to_apply=%region_15.0 | all-reduce | flops 1024 | bytes 4096 | tf_op jit(solution)/shard_map/psum | solution.py:122
  211.8 4.3 %online-softmax = f32[4,256,256]{2,1,0:T(8,128)} custom-call(f32[4,256,256]{2,1,0:T(8,128)} %copy-done, f32[4,256,256]{2,1,0:T(8,128)} %convolution_multiply_fusion.5), custom_call_target="tpu_custom_call" | custom-call | tf_op online-softmax
  216.2 2.6 fusion.77
  220.2 4.3 %online-softmax.1 = f32[4,256,256]{2,1,0:T(8,128)} custom-call(f32[4,256,256]{2,1,0:T(8,128)} %copy-done, f32[4,256,256]{2,1,0:T(8,128)} %convolution_multiply_fusion.4), custom_call_target="tpu_custom_call" | custom-call | tf_op online-softmax
  224.5 2.6 fusion.86
  228.5 4.3 %online-softmax.2 = f32[4,256,256]{2,1,0:T(8,128)} custom-call(f32[4,256,256]{2,1,0:T(8,128)} %copy-done, f32[4,256,256]{2,1,0:T(8,128)} %convolution_multiply_fusion.3), custom_call_target="tpu_custom_call" | custom-call | tf_op online-softmax
  232.8 2.6 fusion.95
  236.8 4.3 %online-softmax.3 = f32[4,256,256]{2,1,0:T(8,128)} custom-call(f32[4,256,256]{2,1,0:T(8,128)} %copy-done, f32[4,256,256]{2,1,0:T(8,128)} %convolution_multiply_fusion.2), custom_call_target="tpu_custom_call" | custom-call | tf_op online-softmax
  241.1 2.6 fusion.104
  245.1 4.3 %online-softmax.4 = f32[4,256,256]{2,1,0:T(8,128)} custom-call(f32[4,256,256]{2,1,0:T(8,128)} %copy-done, f32[4,256,256]{2,1,0:T(8,128)} %convolution_multiply_fusion.1), custom_call_target="tpu_custom_call" | custom-call | tf_op online-softmax
  249.5 2.6 fusion.113
  253.5 6.3 %fusion.13 = f32[4,128,2048]{2,1,0:T(8,128)} fusion(bf16[256,4,128]{2,0,1:T(8,128)(2,1)S(1)} %fusion.124, f32[4,2048,256]{1,2,0:T(8,128)} %get-tuple-element.51, f32[4,2048]{1,0:T(4,128)S(1)} %get-tuple-element.50), kind=kOutput, calls=%fused_computation.54 | convolution fusion | flops 541065216 | bytes 12877824 | tf_op jit(solution)/shard_map/kbv,vkg->bkg/dot_general | solution.py:132
  260.0 5.5 %copy.94 = f32[2048,512]{1,0:T(8,128)} copy(f32[2048,512]{0,1:T(8,128)} %bitcast.121) | data formatting | bytes 8388608 | tf_op jit(solution)/shard_map/reshape | solution.py:134
  265.9 29.8 %add_convert_fusion = bf16[2048,512]{1,0:T(8,128)(2,1)} fusion(f32[2048,512]{1,0:T(8,128)} %copy.94, bf16[2048,512]{1,0:T(8,128)(2,1)S(1)} %copy-done.6, bf16[16,512]{1,0:T(8,128)(2,1)S(1)} %collective-permute-done.1, bf16[16,512]{1,0:T(8,128)(2,1)S(1)} %collective-permute-done, f32[512]{0:T(512)S(1)} %bitcast.132, f32[512]{0:T(512)S(1)} %bitcast.133, ...), kind=kLoop, calls=%fused_computation.44 | loop fusion | flops 205520896 | bytes 8488960 | tf_op jit(solution)/shard_map/convert_element_type | solution.py:145
  (140 shorter events, 26.7 us)
Async XLA Ops:
  51.6 158.4 %copy-start = (f32[4,256,256]{2,1,0:T(8,128)}, f32[4,256,256]{2,1,0:T(8,128)S(1)}, u32[]{:S(2)}) copy-start(f32[4,256,256]{2,1,0:T(8,128)S(1)} %get-tuple-element.47) | copy-start | bytes 3145732
  55.7 150.4 %all-to-all-start = ((f32[8,1,2]{2,1,0:T(1,128)}), f32[8,1,2]{2,1,0:T(1,128)S(1)}, u32[]{:S(2)}, u32[]{:S(2)}) async-start(f32[8,1,2]{2,1,0:T(1,128)} %broadcast_in_dim.4), calls=%async_computation | async-start | bytes 8192 | tf_op jit(solution)/shard_map/all_to_all | solution.py:25
  64.3 187.8 %all-reduce.2.cloned.1.call-start = ((), (), s32[]{:S(2)}) async-start(), calls=%async_computation.1 | async-start | bytes 524288 | tf_op jit(solution)/shard_map/psum | solution.py:123
  68.7 25.4 %copy-start.10 = (f32[2048,4]{0,1:T(4,128)S(1)}, f32[2048,4]{0,1:T(4,128)}, u32[]{:S(2)}) copy-start(f32[2048,4]{0,1:T(4,128)} %param.12) | copy-start | bytes 98308
  102.9 162.7 %collective-permute-start = (bf16[16,512]{1,0:T(8,128)(2,1)S(1)}, bf16[16,512]{1,0:T(8,128)(2,1)S(1)}, u32[]{:S(2)}, u32[]{:S(2)}) collective-permute-start(bf16[16,512]{1,0:T(8,128)(2,1)S(1)} %copy.107), channel_id=1, source_target_pairs={{0,8},{8,16},{16,24},{24,32},{32,40},{40,48},{48,56},{56,64},{64,7... | collective-permute-start | bytes 49160 | tf_op jit(solution)/shard_map/ppermute | solution.py:53
  105.1 160.5 %collective-permute-start.1 = (bf16[16,512]{1,0:T(8,128)(2,1)S(1)}, bf16[16,512]{1,0:T(8,128)(2,1)S(1)}, u32[]{:S(2)}, u32[]{:S(2)}) collective-permute-start(bf16[16,512]{1,0:T(8,128)(2,1)S(1)} %copy.109), channel_id=1, source_target_pairs={{8,0},{16,8},{24,16},{32,24},{40,32},{48,40},{56,48},{64,56},{72,6... | collective-permute-start | bytes 49160 | tf_op jit(solution)/shard_map/ppermute | solution.py:54
  211.8 6.9 %copy-start.8 = (f32[4,256,256]{2,1,0:T(8,128)S(1)}, f32[4,256,256]{2,1,0:T(8,128)}, u32[]{:S(2)}) copy-start(f32[4,256,256]{2,1,0:T(8,128)} %convolution_multiply_fusion.5) | copy-start | bytes 3145732
  220.2 6.9 %copy-start.1 = (f32[4,256,256]{2,1,0:T(8,128)S(1)}, f32[4,256,256]{2,1,0:T(8,128)}, u32[]{:S(2)}) copy-start(f32[4,256,256]{2,1,0:T(8,128)} %convolution_multiply_fusion.4) | copy-start | bytes 3145732
  228.5 6.9 %copy-start.2 = (f32[4,256,256]{2,1,0:T(8,128)S(1)}, f32[4,256,256]{2,1,0:T(8,128)}, u32[]{:S(2)}) copy-start(f32[4,256,256]{2,1,0:T(8,128)} %convolution_multiply_fusion.3) | copy-start | bytes 3145732
  236.8 6.9 %copy-start.3 = (f32[4,256,256]{2,1,0:T(8,128)S(1)}, f32[4,256,256]{2,1,0:T(8,128)}, u32[]{:S(2)}) copy-start(f32[4,256,256]{2,1,0:T(8,128)} %convolution_multiply_fusion.2) | copy-start | bytes 3145732
  245.1 7.0 %copy-start.7 = (f32[4,256,256]{2,1,0:T(8,128)S(1)}, f32[4,256,256]{2,1,0:T(8,128)}, u32[]{:S(2)}) copy-start(f32[4,256,256]{2,1,0:T(8,128)} %convolution_multiply_fusion.1) | copy-start | bytes 3145732
  259.8 5.9 %copy-start.16 = (f32[512,1]{0,1:T(1,128)S(1)}, f32[512,1]{0,1:T(1,128)}, u32[]{:S(2)}) copy-start(f32[512,1]{0,1:T(1,128)} %get-tuple-element.15) | copy-start | bytes 6148
  259.8 5.9 %copy-start.17 = (f32[512,1]{0,1:T(1,128)S(1)}, f32[512,1]{0,1:T(1,128)}, u32[]{:S(2)}) copy-start(f32[512,1]{0,1:T(1,128)} %get-tuple-element.16) | copy-start | bytes 6148
  259.8 5.9 %copy-start.18 = (f32[512,1]{0,1:T(1,128)S(1)}, f32[512,1]{0,1:T(1,128)}, u32[]{:S(2)}) copy-start(f32[512,1]{0,1:T(1,128)} %get-tuple-element.17) | copy-start | bytes 6148
  259.8 5.9 %copy-start.19 = (f32[512,1]{0,1:T(1,128)S(1)}, f32[512,1]{0,1:T(1,128)}, u32[]{:S(2)}) copy-start(f32[512,1]{0,1:T(1,128)} %get-tuple-element.18) | copy-start | bytes 6148
  259.8 5.9 %copy-start.20 = (f32[512,1]{0,1:T(1,128)S(1)}, f32[512,1]{0,1:T(1,128)}, u32[]{:S(2)}) copy-start(f32[512,1]{0,1:T(1,128)} %get-tuple-element.19) | copy-start | bytes 6148
  259.8 5.9 %copy-start.21 = (f32[512,1]{0,1:T(1,128)S(1)}, f32[512,1]{0,1:T(1,128)}, u32[]{:S(2)}) copy-start(f32[512,1]{0,1:T(1,128)} %get-tuple-element.20) | copy-start | bytes 6148
  259.8 5.9 %copy-start.22 = (f32[512,1]{0,1:T(1,128)S(1)}, f32[512,1]{0,1:T(1,128)}, u32[]{:S(2)}) copy-start(f32[512,1]{0,1:T(1,128)} %get-tuple-element.21) | copy-start | bytes 6148
  259.8 5.9 %copy-start.23 = (f32[512,1]{0,1:T(1,128)S(1)}, f32[512,1]{0,1:T(1,128)}, u32[]{:S(2)}) copy-start(f32[512,1]{0,1:T(1,128)} %get-tuple-element.22) | copy-start | bytes 6148
  259.8 5.9 %copy-start.24 = (f32[512,1]{0,1:T(1,128)S(1)}, f32[512,1]{0,1:T(1,128)}, u32[]{:S(2)}) copy-start(f32[512,1]{0,1:T(1,128)} %get-tuple-element.23) | copy-start | bytes 6148
  259.8 5.9 %copy-start.25 = (f32[512,1]{0,1:T(1,128)S(1)}, f32[512,1]{0,1:T(1,128)}, u32[]{:S(2)}) copy-start(f32[512,1]{0,1:T(1,128)} %get-tuple-element.24) | copy-start | bytes 6148
  259.9 5.9 %copy-start.26 = (f32[512,1]{0,1:T(1,128)S(1)}, f32[512,1]{0,1:T(1,128)}, u32[]{:S(2)}) copy-start(f32[512,1]{0,1:T(1,128)} %get-tuple-element.25) | copy-start | bytes 6148
  259.9 5.9 %copy-start.27 = (f32[512,1]{0,1:T(1,128)S(1)}, f32[512,1]{0,1:T(1,128)}, u32[]{:S(2)}) copy-start(f32[512,1]{0,1:T(1,128)} %get-tuple-element.26) | copy-start | bytes 6148
  259.9 5.9 %copy-start.28 = (f32[512,1]{0,1:T(1,128)S(1)}, f32[512,1]{0,1:T(1,128)}, u32[]{:S(2)}) copy-start(f32[512,1]{0,1:T(1,128)} %get-tuple-element.27) | copy-start | bytes 6148
  259.9 5.9 %copy-start.29 = (f32[512,1]{0,1:T(1,128)S(1)}, f32[512,1]{0,1:T(1,128)}, u32[]{:S(2)}) copy-start(f32[512,1]{0,1:T(1,128)} %get-tuple-element.28) | copy-start | bytes 6148
  259.9 5.9 %copy-start.30 = (f32[512,1]{0,1:T(1,128)S(1)}, f32[512,1]{0,1:T(1,128)}, u32[]{:S(2)}) copy-start(f32[512,1]{0,1:T(1,128)} %get-tuple-element.29) | copy-start | bytes 6148
  259.9 5.9 %copy-start.31 = (f32[512,1]{0,1:T(1,128)S(1)}, f32[512,1]{0,1:T(1,128)}, u32[]{:S(2)}) copy-start(f32[512,1]{0,1:T(1,128)} %get-tuple-element.30) | copy-start | bytes 6148
  259.9 5.9 %copy-start.32 = (f32[512,1]{0,1:T(1,128)S(1)}, f32[512,1]{0,1:T(1,128)}, u32[]{:S(2)}) copy-start(f32[512,1]{0,1:T(1,128)} %get-tuple-element.31) | copy-start | bytes 6148
  259.9 5.9 %copy-start.33 = (f32[512,1]{0,1:T(1,128)S(1)}, f32[512,1]{0,1:T(1,128)}, u32[]{:S(2)}) copy-start(f32[512,1]{0,1:T(1,128)} %get-tuple-element.32) | copy-start | bytes 6148
  259.9 5.9 %copy-start.34 = (f32[512,1]{0,1:T(1,128)S(1)}, f32[512,1]{0,1:T(1,128)}, u32[]{:S(2)}) copy-start(f32[512,1]{0,1:T(1,128)} %get-tuple-element.33) | copy-start | bytes 6148
  259.9 5.9 %copy-start.35 = (f32[512,1]{0,1:T(1,128)S(1)}, f32[512,1]{0,1:T(1,128)}, u32[]{:S(2)}) copy-start(f32[512,1]{0,1:T(1,128)} %get-tuple-element.34) | copy-start | bytes 6148
  259.9 5.9 %copy-start.36 = (f32[512,1]{0,1:T(1,128)S(1)}, f32[512,1]{0,1:T(1,128)}, u32[]{:S(2)}) copy-start(f32[512,1]{0,1:T(1,128)} %get-tuple-element.35) | copy-start | bytes 6148
  (18 other events, 96.1 us)
Sparse Core Ops, SparseCore 0:
  102.8 108.5 all-reduce.1
where the time goes:
time: 304 us; the launch traced here: 303 us
  blocking collectives  111 us (37%)
  other arithmetic  66.2 us (22%)
  matrix products  45.7 us (15%)
  local copies, waits for them, and re-layouts  30.2 us (10%)
  Pallas kernels  21.7 us (7%)
  between operations  15.5 us (5%)
  starting transfers between devices  12.1 us (4%)
    psum x1, blocking collectives, shards(): lax.psum(total.astype(jnp.bfloat16), SEQ).astype(jnp.float32)  64.7 us
    convert_element_type x1, other arithmetic, shards(): return (attended + mixed).astype(jnp.bfloat16)  29.8 us
    all_gather x1, blocking collectives, side_by_side(): lax.all_gather(both, axis, axis=dim, tiled=True)  25.1 us
    unnamed x5, Pallas kernels  21.7 us
    pmax x3, blocking collectives, by_axis(): return functools.reduce(lax.pmax, axes, shard)  21.3 us
    dot_general x6, matrix products, newton(): inner_term = 13.0 * eye_matrix - jnp.dot(product, inner_term)  13.4 us
    convert_element_type x3, local copies, waits for them, and re-layouts, dequant(): value_rows.reshape(value_rows.shape[0], count, HEAD_DIM).astype(jnp.float32)  11.9 us
    sub x1, other arithmetic, shards(): local_term = jax.nn.softmax(near_scores, axis=-1).astype(jnp.bfloat16)  11.7 us
  transfers between devices with their start and end apart: 4, of which 0 were waited for; matrix products, arithmetic and copies ran while one was open for 29% of the time, Pallas kernels for 7%

commit v1 on v0

--- a/solution.py
+++ b/solution.py
@@ -75,6 +75,12 @@
 
 
 def shards(q_values, k_values, v_values, q_scales, k_scales, v_scales, conv_weight):
+
+    def _place_rails(array_here):
+        for src_i in ("seq_0", ("seq_1", "seq_2")):
+            array_here = lax.psum(array_here, src_i)
+        return array_here
+
     tok_rows = q_values.shape[0]
     head_count = q_scales.shape[1]
     seq_count = lax.axis_size(SEQ)
@@ -119,7 +125,7 @@
         preferred_element_type=jnp.float32,
     )
     total, summed = (
-        lax.psum(total.astype(jnp.bfloat16), SEQ).astype(jnp.float32),
+        _place_rails(total.astype(jnp.bfloat16)).astype(jnp.float32),
         lax.psum(summed.astype(jnp.bfloat16), SEQ).astype(jnp.float32),
     )
     reduced = summed / jnp.swapaxes(total, 0, 1)[:, :, None]

time: 304 us -> 265 us (0.87)
  blocking collectives: 111 us -> 72.2 us
    psum x1 -> x2, blocking collectives: 64.7 us -> 25.9 us  [_place_rails(): array_here = lax.psum(array_here, src_i)]
  transfers between devices with their start and end apart: 4 -> 4, of which waited for: 0 -> 0; matrix products, arithmetic and copies ran while one was open for 29% -> 33% of each run, Pallas kernels for 7% -> 8%
where the time goes in v1:
time: 265 us; the launch traced here: 263 us
  blocking collectives  72.2 us (27%)
  other arithmetic  66.1 us (25%)
  matrix products  45.3 us (17%)
  local copies, waits for them, and re-layouts  30.3 us (11%)
  Pallas kernels  21.5 us (8%)
  between operations  15.6 us (6%)
  starting transfers between devices  11.9 us (4%)
    convert_element_type x1, other arithmetic, shards(): return (attended + mixed).astype(jnp.bfloat16)  29.8 us
    psum x2, blocking collectives, _place_rails(): array_here = lax.psum(array_here, src_i)  25.9 us
    all_gather x1, blocking collectives, side_by_side(): lax.all_gather(both, axis, axis=dim, tiled=True)  25.1 us
    unnamed x5, Pallas kernels  21.5 us
    pmax x3, blocking collectives, by_axis(): return functools.reduce(lax.pmax, axes, shard)  21.3 us
    dot_general x6, matrix products, newton(): inner_term = 13.0 * eye_matrix - jnp.dot(product, inner_term)  13.2 us
    convert_element_type x3, local copies, waits for them, and re-layouts, dequant(): value_rows.reshape(value_rows.shape[0], count, HEAD_DIM).astype(jnp.float32)  11.9 us
    sub x1, other arithmetic, shards(): local_term = jax.nn.softmax(near_scores, axis=-1).astype(jnp.bfloat16)  11.7 us
  transfers between devices with their start and end apart: 4, of which 0 were waited for; matrix products, arithmetic and copies ran while one was open for 33% of the time, Pallas kernels for 8%

profile of v1, /device:TPU:32, one launch (start us, length us, event | category | flops | bytes accessed | tf_op | source)
XLA Modules:
  0.0 263.0 jit_solution(11794737422688161686)
XLA Ops:
  6.5 4.7 %reshape.126 = f32[8,256,4,128]{3,2,1,0:T(4,128)} reshape(bf16[2048,512]{1,0:T(8,128)(2,1)} %param.7) | data formatting | bytes 6291456 | tf_op jit(solution)/shard_map/convert_element_type | solution.py:61
  11.6 4.6 %convert_reduce_fusion.1 = f32[8,4,128]{2,1,0:T(4,128)S(1)} fusion(f32[8,256,4,128]{3,2,1,0:T(4,128)} %reshape.126, f32[8,256,4]{2,1,0:T(8,128)S(1)} %bitcast.117), kind=kLoop, calls=%fused_computation.52 | loop fusion | flops 4190208 | bytes 4243456 | tf_op jit(solution)/shard_map/reduce_sum | solution.py:96
  16.2 3.0 %reshape.127 = f32[8,256,4,128]{3,2,1,0:T(4,128)} reshape(bf16[2048,512]{1,0:T(8,128)(2,1)S(1)} %copy-done.4) | data formatting | bytes 6291456 | tf_op jit(solution)/shard_map/convert_element_type | solution.py:61
  19.6 4.4 %convert_reduce_fusion = f32[8,4,128]{2,1,0:T(4,128)S(1)} fusion(f32[8,256,4,128]{3,2,1,0:T(4,128)} %reshape.127, f32[8,256,4]{2,1,0:T(8,128)S(1)} %bitcast.118), kind=kLoop, calls=%fused_computation.50 | loop fusion | flops 4190208 | bytes 4243456 | tf_op jit(solution)/shard_map/reduce_sum | solution.py:96
  24.1 25.1 %all_gather.3 = bf16[256,1024]{1,0:T(8,128)(2,1)S(1)} all-gather(bf16[8,1024]{1,0:T(8,128)(2,1)S(1)} %pad_maximum_fusion.2), channel_id=1, replica_groups=mesh['seq_0'=4,'seq_1'=4,'seq_2'=2,'head'=8] {'seq_0','seq_1','seq_2'}, dimensions={0}, use_global_device_ids=true | all-gather | bytes 540672 | tf_op jit(solution)/shard_map/all_gather | solution.py:16
  55.7 8.6 %all-to-all-start = ((f32[8,1,2]{2,1,0:T(1,128)}), f32[8,1,2]{2,1,0:T(1,128)S(1)}, u32[]{:S(2)}, u32[]{:S(2)}) async-start(f32[8,1,2]{2,1,0:T(1,128)} %broadcast_in_dim.4), calls=%async_computation | async-start | bytes 8192 | tf_op jit(solution)/shard_map/all_to_all | solution.py:25
  64.3 4.4 %multiply_reduce_fusion = (f32[4,256]{1,0:T(4,128)S(1)}, f32[4,256,2048]{2,1,0:T(8,128)}) fusion(bf16[256,4,128]{0,2,1:T(8,128)(2,1)S(1)} %bitcast.121, f32[2048,4]{0,1:T(4,128)S(1)} %copy-done.11, bf16[2048,512]{1,0:T(8,128)(2,1)S(1)} %copy-done.4), kind=kOutput, calls=%fused_computation.34 | convolution fusion | flops 544209920 | bytes 10784768 | tf_op jit(solution)/shard_map/kli,nli->lkn/dot_general | solution.py:115
  68.7 10.2 %pmax.21 = f32[4,256]{1,0:T(4,128)S(1)} all-reduce(f32[4,256]{1,0:T(4,128)S(1)} %get-tuple-element.48), channel_id=1, replica_groups=mesh['seq_0'=4,'seq_1'=4,'seq_2'=2,'head'=8] {'seq_0'}, use_global_device_ids=true, to_apply=%region_10.0 | all-reduce | flops 1024 | bytes 8192 | tf_op jit(solution)/shard_map/pmax | solution.py:43
  78.9 8.6 %pmax.22 = f32[4,256]{1,0:T(4,128)S(1)} all-reduce(f32[4,256]{1,0:T(4,128)S(1)} %pmax.21), channel_id=1, replica_groups=mesh['seq_0'=4,'seq_1'=4,'seq_2'=2,'head'=8] {'seq_1'}, use_global_device_ids=true, to_apply=%region_11.0 | all-reduce | flops 1024 | bytes 8192 | tf_op jit(solution)/shard_map/pmax | solution.py:43
  89.9 4.2 %copy.106 = f32[2048,512]{0,1:T(8,128)} copy(bf16[2048,512]{1,0:T(8,128)(2,1)} %param.9) | data formatting | bytes 6291456 | tf_op jit(solution)/shard_map/convert_element_type | solution.py:61
  94.1 2.7 %multiply_convert_fusion.1 = bf16[2048,4,128]{0,2,1:T(8,128)(2,1)S(1)} fusion(f32[2048,4,128]{0,2,1:T(8,128)} %bitcast.115, f32[2048,4]{0,1:T(4,128)S(1)} %copy-done.10), kind=kLoop, calls=%fused_computation.49 | loop fusion | flops 2097152 | bytes 6324224 | tf_op jit(solution)/shard_map/convert_element_type | solution.py:62
  96.8 5.9 %fusion.121 = bf16[256,4,128]{0,2,1:T(8,128)(2,1)} fusion(bf16[2048,4,128]{0,2,1:T(8,128)(2,1)S(1)} %multiply_convert_fusion.1, f32[4,256,2048]{2,1,0:T(8,128)} %get-tuple-element.49, f32[4,256]{1,0:T(4,128)S(1)} %pmax.23), kind=kOutput, calls=%fused_computation.148 | convolution fusion | flops 543293440 | bytes 10752000 | tf_op jit(solution)/shard_map/lnx,xlj->nlj/dot_general | solution.py:121
  106.5 4.4 %fusion.2 = bf16[4,256]{1,0:T(4,128)(2,1)S(1)} fusion(f32[4,256,2048]{2,1,0:T(8,128)} %get-tuple-element.49, f32[4,256]{1,0:T(4,128)S(1)} %pmax.23), kind=kLoop, calls=%fused_computation.37 | loop fusion | flops 6290432 | bytes 8394752 | tf_op jit(solution)/shard_map/reduce_sum | solution.py:120
  110.9 4.2 %fusion.16 = f32[4,2048,256]{1,2,0:T(8,128)} fusion(bf16[256,4,128]{0,2,1:T(8,128)(2,1)S(1)} %bitcast.123, f32[2048,4]{0,1:T(4,128)S(1)} %copy-done.12, bf16[2048,512]{1,0:T(8,128)(2,1)S(1)} %copy-done.5), kind=kOutput, calls=%fused_computation.56 | convolution fusion | flops 540016640 | bytes 10780672 | tf_op jit(solution)/shard_map/zea,uea->ezu/dot_general | solution.py:134
  116.7 13.5 %psum.22 = bf16[4,256]{1,0:T(4,128)(2,1)S(1)} all-reduce(bf16[4,256]{1,0:T(4,128)(2,1)S(1)} %fusion.2), channel_id=1, replica_groups=mesh['seq_0'=4,'seq_1'=4,'seq_2'=2,'head'=8] {'seq_0'}, use_global_device_ids=true, to_apply=%region_15.0 | all-reduce | flops 1024 | bytes 4096 | tf_op jit(solution)/shard_map/psum | solution.py:81
  130.2 11.7 %fusion.170 = (f32[4,2048]{1,0:T(4,128)S(1)}, f32[4,2048,256]{1,2,0:T(8,128)}) fusion(f32[4,2048,256]{1,2,0:T(8,128)} %fusion.16), kind=kOutput, calls=%fused_computation.198 | output fusion | flops 8388863 | bytes 16809984 | tf_op jit(solution)/shard_map/sub | solution.py:137
  144.4 5.4 %copy.108 = f32[2048,512]{1,0:T(8,128)} copy(f32[2048,512]{0,1:T(8,128)} %bitcast.116) | data formatting | bytes 8388608 | tf_op jit(solution)/shard_map/mul | solution.py:62
  149.8 4.9 %multiply_convert_fusion = bf16[2048,512]{1,0:T(8,128)(2,1)} fusion(f32[2048,512]{1,0:T(8,128)} %copy.108, bf16[2048,512]{1,0:T(8,128)(2,1)} %param.9), kind=kLoop, calls=%fused_computation.45 | loop fusion | flops 3145728 | bytes 8388608 | tf_op jit(solution)/shard_map/convert_element_type | solution.py:62
  154.7 12.4 %psum.23 = bf16[256,4]{0,1:T(4,128)(2,1)S(1)} all-reduce(bf16[256,4]{0,1:T(4,128)(2,1)S(1)} %bitcast.162), channel_id=1, replica_groups=mesh['seq_0'=4,'seq_1'=4,'seq_2'=2,'head'=8] {'seq_1','seq_2'}, use_global_device_ids=true, to_apply=%region_16.0 | all-reduce | flops 1024 | bytes 4096 | tf_op jit(solution)/shard_map/psum | solution.py:81
  172.8 4.3 %online-softmax = f32[4,256,256]{2,1,0:T(8,128)} custom-call(f32[4,256,256]{2,1,0:T(8,128)} %copy-done, f32[4,256,256]{2,1,0:T(8,128)} %convolution_multiply_fusion.5), custom_call_target="tpu_custom_call" | custom-call | tf_op online-softmax
  177.1 2.5 fusion.77
  181.0 4.3 %online-softmax.1 = f32[4,256,256]{2,1,0:T(8,128)} custom-call(f32[4,256,256]{2,1,0:T(8,128)} %copy-done, f32[4,256,256]{2,1,0:T(8,128)} %convolution_multiply_fusion.4), custom_call_target="tpu_custom_call" | custom-call | tf_op online-softmax
  185.3 2.5 fusion.86
  189.2 4.3 %online-softmax.2 = f32[4,256,256]{2,1,0:T(8,128)} custom-call(f32[4,256,256]{2,1,0:T(8,128)} %copy-done, f32[4,256,256]{2,1,0:T(8,128)} %convolution_multiply_fusion.3), custom_call_target="tpu_custom_call" | custom-call | tf_op online-softmax
  193.5 2.5 fusion.95
  197.4 4.3 %online-softmax.3 = f32[4,256,256]{2,1,0:T(8,128)} custom-call(f32[4,256,256]{2,1,0:T(8,128)} %copy-done, f32[4,256,256]{2,1,0:T(8,128)} %convolution_multiply_fusion.2), custom_call_target="tpu_custom_call" | custom-call | tf_op online-softmax
  201.7 2.5 fusion.104
  205.6 4.3 %online-softmax.4 = f32[4,256,256]{2,1,0:T(8,128)} custom-call(f32[4,256,256]{2,1,0:T(8,128)} %copy-done, f32[4,256,256]{2,1,0:T(8,128)} %convolution_multiply_fusion.1), custom_call_target="tpu_custom_call" | custom-call | tf_op online-softmax
  209.9 2.5 fusion.113
  213.9 6.3 %fusion.13 = f32[4,128,2048]{2,1,0:T(8,128)} fusion(bf16[256,4,128]{2,0,1:T(8,128)(2,1)S(1)} %fusion.124, f32[4,2048,256]{1,2,0:T(8,128)} %get-tuple-element.51, f32[4,2048]{1,0:T(4,128)S(1)} %get-tuple-element.50), kind=kOutput, calls=%fused_computation.54 | convolution fusion | flops 541065216 | bytes 12877824 | tf_op jit(solution)/shard_map/kbv,vkg->bkg/dot_general | solution.py:138
  220.5 5.5 %copy.94 = f32[2048,512]{1,0:T(8,128)} copy(f32[2048,512]{0,1:T(8,128)} %bitcast.119) | data formatting | bytes 8388608 | tf_op jit(solution)/shard_map/reshape | solution.py:140
  226.3 29.8 %add_convert_fusion = bf16[2048,512]{1,0:T(8,128)(2,1)} fusion(f32[2048,512]{1,0:T(8,128)} %copy.94, bf16[2048,512]{1,0:T(8,128)(2,1)S(1)} %copy-done.6, bf16[16,512]{1,0:T(8,128)(2,1)S(1)} %collective-permute-done.1, bf16[16,512]{1,0:T(8,128)(2,1)S(1)} %collective-permute-done, f32[512]{0:T(512)S(1)} %bitcast.130, f32[512]{0:T(512)S(1)} %bitcast.131, ...), kind=kLoop, calls=%fused_computation.44 | loop fusion | flops 205520896 | bytes 8488960 | tf_op jit(solution)/shard_map/convert_element_type | solution.py:151
  (141 shorter events, 28.8 us)
Async XLA Ops:
  51.6 119.4 %copy-start = (f32[4,256,256]{2,1,0:T(8,128)}, f32[4,256,256]{2,1,0:T(8,128)S(1)}, u32[]{:S(2)}) copy-start(f32[4,256,256]{2,1,0:T(8,128)S(1)} %get-tuple-element.47) | copy-start | bytes 3145732
  55.7 111.4 %all-to-all-start = ((f32[8,1,2]{2,1,0:T(1,128)}), f32[8,1,2]{2,1,0:T(1,128)S(1)}, u32[]{:S(2)}, u32[]{:S(2)}) async-start(f32[8,1,2]{2,1,0:T(1,128)} %broadcast_in_dim.4), calls=%async_computation | async-start | bytes 8192 | tf_op jit(solution)/shard_map/all_to_all | solution.py:25
  64.3 148.3 %all-reduce.2.cloned.1.call-start = ((), (), s32[]{:S(2)}) async-start(), calls=%async_computation.1 | async-start | bytes 524288 | tf_op jit(solution)/shard_map/psum | solution.py:129
  68.7 25.4 %copy-start.10 = (f32[2048,4]{0,1:T(4,128)S(1)}, f32[2048,4]{0,1:T(4,128)}, u32[]{:S(2)}) copy-start(f32[2048,4]{0,1:T(4,128)} %param.12) | copy-start | bytes 98308
  102.9 123.1 %collective-permute-start = (bf16[16,512]{1,0:T(8,128)(2,1)S(1)}, bf16[16,512]{1,0:T(8,128)(2,1)S(1)}, u32[]{:S(2)}, u32[]{:S(2)}) collective-permute-start(bf16[16,512]{1,0:T(8,128)(2,1)S(1)} %copy.107), channel_id=1, source_target_pairs={{0,8},{8,16},{16,24},{24,32},{32,40},{40,48},{48,56},{56,64},{64,7... | collective-permute-start | bytes 49160 | tf_op jit(solution)/shard_map/ppermute | solution.py:53
  105.1 120.9 %collective-permute-start.1 = (bf16[16,512]{1,0:T(8,128)(2,1)S(1)}, bf16[16,512]{1,0:T(8,128)(2,1)S(1)}, u32[]{:S(2)}, u32[]{:S(2)}) collective-permute-start(bf16[16,512]{1,0:T(8,128)(2,1)S(1)} %copy.109), channel_id=1, source_target_pairs={{8,0},{16,8},{24,16},{32,24},{40,32},{48,40},{56,48},{64,56},{72,6... | collective-permute-start | bytes 49160 | tf_op jit(solution)/shard_map/ppermute | solution.py:54
  172.8 6.8 %copy-start.8 = (f32[4,256,256]{2,1,0:T(8,128)S(1)}, f32[4,256,256]{2,1,0:T(8,128)}, u32[]{:S(2)}) copy-start(f32[4,256,256]{2,1,0:T(8,128)} %convolution_multiply_fusion.5) | copy-start | bytes 3145732
  181.0 6.8 %copy-start.1 = (f32[4,256,256]{2,1,0:T(8,128)S(1)}, f32[4,256,256]{2,1,0:T(8,128)}, u32[]{:S(2)}) copy-start(f32[4,256,256]{2,1,0:T(8,128)} %convolution_multiply_fusion.4) | copy-start | bytes 3145732
  189.2 6.8 %copy-start.2 = (f32[4,256,256]{2,1,0:T(8,128)S(1)}, f32[4,256,256]{2,1,0:T(8,128)}, u32[]{:S(2)}) copy-start(f32[4,256,256]{2,1,0:T(8,128)} %convolution_multiply_fusion.3) | copy-start | bytes 3145732
  197.4 6.9 %copy-start.3 = (f32[4,256,256]{2,1,0:T(8,128)S(1)}, f32[4,256,256]{2,1,0:T(8,128)}, u32[]{:S(2)}) copy-start(f32[4,256,256]{2,1,0:T(8,128)} %convolution_multiply_fusion.2) | copy-start | bytes 3145732
  205.6 6.9 %copy-start.7 = (f32[4,256,256]{2,1,0:T(8,128)S(1)}, f32[4,256,256]{2,1,0:T(8,128)}, u32[]{:S(2)}) copy-start(f32[4,256,256]{2,1,0:T(8,128)} %convolution_multiply_fusion.1) | copy-start | bytes 3145732
  220.2 5.8 %copy-start.16 = (f32[512,1]{0,1:T(1,128)S(1)}, f32[512,1]{0,1:T(1,128)}, u32[]{:S(2)}) copy-start(f32[512,1]{0,1:T(1,128)} %get-tuple-element.15) | copy-start | bytes 6148
  220.2 5.8 %copy-start.17 = (f32[512,1]{0,1:T(1,128)S(1)}, f32[512,1]{0,1:T(1,128)}, u32[]{:S(2)}) copy-start(f32[512,1]{0,1:T(1,128)} %get-tuple-element.16) | copy-start | bytes 6148
  220.2 5.8 %copy-start.18 = (f32[512,1]{0,1:T(1,128)S(1)}, f32[512,1]{0,1:T(1,128)}, u32[]{:S(2)}) copy-start(f32[512,1]{0,1:T(1,128)} %get-tuple-element.17) | copy-start | bytes 6148
  220.2 5.8 %copy-start.19 = (f32[512,1]{0,1:T(1,128)S(1)}, f32[512,1]{0,1:T(1,128)}, u32[]{:S(2)}) copy-start(f32[512,1]{0,1:T(1,128)} %get-tuple-element.18) | copy-start | bytes 6148
  220.2 5.8 %copy-start.20 = (f32[512,1]{0,1:T(1,128)S(1)}, f32[512,1]{0,1:T(1,128)}, u32[]{:S(2)}) copy-start(f32[512,1]{0,1:T(1,128)} %get-tuple-element.19) | copy-start | bytes 6148
  220.2 5.8 %copy-start.21 = (f32[512,1]{0,1:T(1,128)S(1)}, f32[512,1]{0,1:T(1,128)}, u32[]{:S(2)}) copy-start(f32[512,1]{0,1:T(1,128)} %get-tuple-element.20) | copy-start | bytes 6148
  220.3 5.8 %copy-start.22 = (f32[512,1]{0,1:T(1,128)S(1)}, f32[512,1]{0,1:T(1,128)}, u32[]{:S(2)}) copy-start(f32[512,1]{0,1:T(1,128)} %get-tuple-element.21) | copy-start | bytes 6148
  220.3 5.8 %copy-start.23 = (f32[512,1]{0,1:T(1,128)S(1)}, f32[512,1]{0,1:T(1,128)}, u32[]{:S(2)}) copy-start(f32[512,1]{0,1:T(1,128)} %get-tuple-element.22) | copy-start | bytes 6148
  220.3 5.8 %copy-start.24 = (f32[512,1]{0,1:T(1,128)S(1)}, f32[512,1]{0,1:T(1,128)}, u32[]{:S(2)}) copy-start(f32[512,1]{0,1:T(1,128)} %get-tuple-element.23) | copy-start | bytes 6148
  220.3 5.8 %copy-start.25 = (f32[512,1]{0,1:T(1,128)S(1)}, f32[512,1]{0,1:T(1,128)}, u32[]{:S(2)}) copy-start(f32[512,1]{0,1:T(1,128)} %get-tuple-element.24) | copy-start | bytes 6148
  220.3 5.8 %copy-start.26 = (f32[512,1]{0,1:T(1,128)S(1)}, f32[512,1]{0,1:T(1,128)}, u32[]{:S(2)}) copy-start(f32[512,1]{0,1:T(1,128)} %get-tuple-element.25) | copy-start | bytes 6148
  220.3 5.8 %copy-start.27 = (f32[512,1]{0,1:T(1,128)S(1)}, f32[512,1]{0,1:T(1,128)}, u32[]{:S(2)}) copy-start(f32[512,1]{0,1:T(1,128)} %get-tuple-element.26) | copy-start | bytes 6148
  220.3 5.8 %copy-start.28 = (f32[512,1]{0,1:T(1,128)S(1)}, f32[512,1]{0,1:T(1,128)}, u32[]{:S(2)}) copy-start(f32[512,1]{0,1:T(1,128)} %get-tuple-element.27) | copy-start | bytes 6148
  220.3 5.8 %copy-start.29 = (f32[512,1]{0,1:T(1,128)S(1)}, f32[512,1]{0,1:T(1,128)}, u32[]{:S(2)}) copy-start(f32[512,1]{0,1:T(1,128)} %get-tuple-element.28) | copy-start | bytes 6148
  220.3 5.8 %copy-start.30 = (f32[512,1]{0,1:T(1,128)S(1)}, f32[512,1]{0,1:T(1,128)}, u32[]{:S(2)}) copy-start(f32[512,1]{0,1:T(1,128)} %get-tuple-element.29) | copy-start | bytes 6148
  220.3 5.8 %copy-start.31 = (f32[512,1]{0,1:T(1,128)S(1)}, f32[512,1]{0,1:T(1,128)}, u32[]{:S(2)}) copy-start(f32[512,1]{0,1:T(1,128)} %get-tuple-element.30) | copy-start | bytes 6148
  220.4 5.8 %copy-start.32 = (f32[512,1]{0,1:T(1,128)S(1)}, f32[512,1]{0,1:T(1,128)}, u32[]{:S(2)}) copy-start(f32[512,1]{0,1:T(1,128)} %get-tuple-element.31) | copy-start | bytes 6148
  220.4 5.8 %copy-start.33 = (f32[512,1]{0,1:T(1,128)S(1)}, f32[512,1]{0,1:T(1,128)}, u32[]{:S(2)}) copy-start(f32[512,1]{0,1:T(1,128)} %get-tuple-element.32) | copy-start | bytes 6148
  220.4 5.8 %copy-start.34 = (f32[512,1]{0,1:T(1,128)S(1)}, f32[512,1]{0,1:T(1,128)}, u32[]{:S(2)}) copy-start(f32[512,1]{0,1:T(1,128)} %get-tuple-element.33) | copy-start | bytes 6148
  220.4 5.8 %copy-start.35 = (f32[512,1]{0,1:T(1,128)S(1)}, f32[512,1]{0,1:T(1,128)}, u32[]{:S(2)}) copy-start(f32[512,1]{0,1:T(1,128)} %get-tuple-element.34) | copy-start | bytes 6148
  220.4 5.8 %copy-start.36 = (f32[512,1]{0,1:T(1,128)S(1)}, f32[512,1]{0,1:T(1,128)}, u32[]{:S(2)}) copy-start(f32[512,1]{0,1:T(1,128)} %get-tuple-element.35) | copy-start | bytes 6148
  (18 other events, 96.1 us)
Sparse Core Ops, SparseCore 0:
  102.8 108.5 all-reduce.1
